TPU v7x, 32 devices: a whole 2x2x4 slice. The times are simulated.
32 devices in a mesh: parts: 2 (over y), tm: 4 (over z), factor: 4 (over x, core).
Axes of the slice: x: 2, y: 2, z: 4, core: 2. Of those that a mesh axis runs over, the one named last changes fastest.
Arguments:
- schur_matrix: float32 [24576, 24, 4, 128], P(('parts', 'tm'), None, 'factor'), parts along dimension 0, as said below
- link_rhs: float32 [24576], P(('parts', 'tm')), parts along dimension 0, may hold values from -6 to 6
- hour_rhs: float32 [32, 256], P(('parts', 'tm', 'factor')), parts along dimension 0, may hold values from -6 to 6
- link_cols: int32 [32, 256], P(('parts', 'tm', 'factor')), parts along dimension 0, may hold values from 0 to 255
- link_coef: float32 [32, 256], P(('parts', 'tm', 'factor')), parts along dimension 0, may hold values from -6 to 6
- hour_inverse: float32 [32, 256, 256], P(('parts', 'tm', 'factor')), parts along dimension 0, may hold values from -0.375 to 0.375
- couple_prev: float32 [32, 2, 256], P(('parts', 'tm', 'factor')), parts along dimension 0, may hold values from -1.2 to 1.2
- couple_next: float32 [32, 2, 256], P(('parts', 'tm', 'factor')), parts along dimension 0, may hold values from -1.2 to 1.2
Outputs:
- schur_trail: float32 [24576, 24, 4, 128], P(('parts', 'tm'), None, 'factor'), parts along dimension 0
- link_trail: float32 [24576], P(('parts', 'tm')), parts along dimension 0
- hour_step: float32 [32, 256], P(('parts', 'tm', 'factor')), parts along dimension 0
There are 2 independent parts, one for each index of `parts`. A program takes and returns all parts, laid end to end along the dimension named above; each array names one. Nothing has to cross between parts.
Inputs may be any that keep to these rules, and one draw needn't show every extreme that they name: schur_matrix is symmetric and its leading 2 * 128 rows and columns form a positive definite block.
All inputs are finite; a program needn't handle non-finite values.
Results may differ from a plain program's by a relative error of at most 0.0001.
Values sent between devices are 32-bit elements; how exact they have to be, the bound alone decides.
A program may use at most 192 MiB of HBM per device.

v0:
```python
import jax
import jax.numpy as jnp
from jax import lax
from jax.sharding import PartitionSpec as P

PANELS = 2
BW = 2
SWEEPS = 2


def spread(array, axis, root):
    mine = lax.axis_index(axis) == root
    return lax.psum(jnp.where(mine, array, jnp.zeros_like(array)), axis)


def with_halo(cells, sides, width):
    for axis, dim in sides:
        count = lax.axis_size(axis)
        ends = count - 1
        head = lax.slice_in_dim(cells, 0, width, axis=dim)
        tail = lax.slice_in_dim(cells, cells.shape[dim] - width, cells.shape[dim], axis=dim)
        cells = jnp.concatenate(
            [
                lax.ppermute(tail, axis, [(i, (i + 1) % count) for i in range(ends)]),
                cells,
                lax.ppermute(head, axis, [((i + 1) % count, i) for i in range(ends)]),
            ],
            axis=dim,
        )
    return cells


def shards(
    schur_matrix, link_rhs, hour_rhs, link_cols, link_coef, hour_inverse, couple_prev, couple_next
):
    rows_here = schur_matrix.shape[0]
    tiles_here = schur_matrix.shape[1]
    width = schur_matrix.shape[3]
    factors = lax.axis_size("factor")
    row_start = lax.axis_index("tm") * rows_here
    global_rows = row_start + jnp.arange(rows_here, dtype=jnp.int32)
    factor_here = lax.axis_index("factor")
    schur_now = schur_matrix
    rhs_now = link_rhs
    solved = []
    for panel_id in range(PANELS):
        column_tile = panel_id // factors
        owner_index = panel_id % factors
        own_cols = schur_now[:, column_tile, 0, :]
        panel_cols = spread(own_cols, "factor", owner_index)
        panel_first = panel_id * width
        picker = (
            global_rows[:, None] - panel_first == jnp.arange(width, dtype=jnp.int32)[None, :]
        ).astype(jnp.float32)
        block_part = jnp.dot(picker.T, panel_cols, precision=lax.Precision.HIGHEST)
        rhs_part = jnp.dot(picker.T, rhs_now, precision=lax.Precision.HIGHEST)
        diag_block, rhs_segment = lax.psum((block_part, rhs_part), "tm")
        lower_block = jnp.linalg.cholesky(diag_block)
        factor_rows = jax.scipy.linalg.solve_triangular(lower_block, panel_cols.T, lower=True).T
        factor_rows = jnp.where(
            (global_rows < panel_first)[:, None], jnp.zeros_like(factor_rows), factor_rows
        )
        all_factor = lax.all_gather(factor_rows, "tm", axis=0, tiled=True)
        grouped = all_factor.reshape(tiles_here, factors, width, width)
        my_tiles = lax.dynamic_index_in_dim(grouped, factor_here, 1, keepdims=False)
        link_step = jax.scipy.linalg.solve_triangular(lower_block, rhs_segment, lower=True)
        rhs_now = rhs_now - jnp.dot(factor_rows, link_step, precision=lax.Precision.HIGHEST)
        update = jnp.einsum("rk,tck->rtc", factor_rows, my_tiles, precision=lax.Precision.HIGHEST)
        schur_now = schur_now - update[:, :, None, :]
        solved.append(link_step)
    link_values = jnp.concatenate(solved)
    one_hot = (
        link_cols[:, :, None] == jnp.arange(PANELS * width, dtype=jnp.int32)[None, None, :]
    ).astype(jnp.float32)
    looked = jnp.einsum("hik,k->hi", one_hot, link_values, precision=lax.Precision.HIGHEST)
    target = hour_rhs - link_coef * looked
    hour_state = jnp.einsum("hik,hk->hi", hour_inverse, target, precision=lax.Precision.HIGHEST)
    for sweep_id in range(SWEEPS):
        border_pairs = jnp.concatenate((hour_state[:, :BW], hour_state[:, -BW:]), axis=1)
        padded = with_halo(border_pairs, ((("tm", "factor"), 0),), 1)
        prev_last = padded[:-2, BW:]
        next_first = padded[2:, :BW]
        coupling = jnp.einsum("hbi,hb->hi", couple_prev, prev_last, precision=lax.Precision.HIGHEST)
        coupling = coupling + jnp.einsum(
            "hbi,hb->hi", couple_next, next_first, precision=lax.Precision.HIGHEST
        )
        hour_state = jnp.einsum(
            "hik,hk->hi", hour_inverse, target - coupling, precision=lax.Precision.HIGHEST
        )
    return (schur_now, rhs_now, hour_state)


def solution(mesh):
    placed = (
        P(("parts", "tm"), None, "factor", None),
        P(("parts", "tm")),
        P(("parts", "tm", "factor"), None),
        P(("parts", "tm", "factor"), None),
        P(("parts", "tm", "factor"), None),
        P(("parts", "tm", "factor"), None, None),
        P(("parts", "tm", "factor"), None, None),
        P(("parts", "tm", "factor"), None, None),
    )
    return jax.shard_map(
        shards,
        mesh=mesh,
        in_specs=placed,
        out_specs=(
            P(("parts", "tm"), None, "factor", None),
            P(("parts", "tm")),
            P(("parts", "tm", "factor"), None),
        ),
        check_vma=False,
    )
```

profile of v0, /device:TPU:0, one launch (start us, length us, event | category | flops | bytes accessed | tf_op | source)
XLA Modules:
  0.0 661.5 jit_solution(964721345408237185)
XLA Ops:
  7.2 32.9 %copy.16 = f32[3072,24,1,128]{3,0,1,2:T(8,128)} copy(f32[3072,24,1,128]{3,2,1,0:T(1,128)} %param.13) | data formatting | bytes 75497472 | tf_op args[0]
  42.9 45.6 %all-reduce.5.cloned.1.call-done = f32[3072,128]{1,0:T(8,128)} async-done(((f32[3072,128]{1,0:T(8,128)}), f32[3072,128]{1,0:T(8,128)}) %all-reduce.5.cloned.1.call-update) | async-done | bytes 1572880 | tf_op jit(solution)/shard_map/psum | solution.py:13
  88.6 4.0 fusion.8
  92.6 34.1 %all-reduce.7.cloned.1.call-done = f32[128,128]{0,1:T(8,128)} async-done(((f32[128,128]{0,1:T(8,128)}), f32[128,128]{0,1:T(8,128)}) %all-reduce.7.cloned.1.call-update) | async-done | bytes 65552 | tf_op jit(solution)/shard_map/psum | solution.py:57
  128.6 11.7 %cholesky.44 = f32[128,128]{1,0:T(8,128)S(1)} custom-call(f32[128,128]{1,0:T(8,128)S(1)} %fusion.35), custom_call_target="Cholesky" | custom-call | tf_op jit(solution)/shard_map/jit(cholesky)/cholesky | solution.py:58
  141.6 9.8 %custom-call.10 = f32[1,128,128]{1,2,0:T(8,128)S(1)} custom-call(f32[1,128,128]{2,1,0:T(8,128)S(1)} %fusion.26), custom_call_target="InvertDiagBlocksLowerTriangular" | custom-call | tf_op jit(solution)/shard_map/jit(_solve_triangular)/triangular_solve | solution.py:59
  154.7 114.7 %all-gather.3.cloned.1.call-done = f32[12288,128]{0,1:T(8,128)} async-done(((f32[3072,128]{0,1:T(8,128)}), f32[12288,128]{0,1:T(8,128)}) %all-gather.3.cloned.1.call-update) | async-done | bytes 6291472 | tf_op jit(solution)/shard_map/all_gather | solution.py:63
  269.3 8.3 %reshape.109 = f32[24,4,128,128]{2,1,0,3:T(4,128)} reshape(f32[12288,128]{0,1:T(8,128)} %all-gather.3.cloned.1.call-done) | data formatting | bytes 12582912 | tf_op jit(solution)/shard_map/reshape | solution.py:64
  277.7 5.6 constant_dynamic-slice_fusion.1
  283.2 3.8 copy.14
  287.1 41.2 %bitcast_subtract_fusion.1 = f32[3072,24,1,128]{3,0,1,2:T(8,128)} fusion(f32[24,1,128,128]{3,2,0,1:T(8,128)S(1)} %copy.14, f32[128,3072]{1,0:T(8,128)S(1)} %copy-done.3, f32[3072,24,1,128]{3,2,1,0:T(1,128)} %param.13), kind=kOutput, calls=%fused_computation.1 | convolution fusion | flops 14504951808 | bytes 78643200 | tf_op jit(solution)/shard_map/rk,tck->rtc/dot_general | solution.py:68
  331.1 41.1 %all-reduce.9.cloned.1.call-done = f32[3072,128]{1,0:T(8,128)} async-done(((f32[3072,128]{1,0:T(8,128)}), f32[3072,128]{1,0:T(8,128)}) %all-reduce.9.cloned.1.call-update) | async-done | bytes 1572880 | tf_op jit(solution)/shard_map/psum | solution.py:13
  372.2 4.0 fusion.9
  376.5 34.0 %all-reduce.11.cloned.1.call-done = f32[128,128]{0,1:T(8,128)} async-done(((f32[128,128]{0,1:T(8,128)}), f32[128,128]{0,1:T(8,128)}) %all-reduce.11.cloned.1.call-update) | async-done | bytes 65552 | tf_op jit(solution)/shard_map/psum | solution.py:57
  412.9 12.5 %cholesky.55 = f32[128,128]{1,0:T(8,128)S(1)} custom-call(f32[128,128]{1,0:T(8,128)} %fusion.31), custom_call_target="Cholesky" | custom-call | tf_op jit(solution)/shard_map/jit(cholesky)/cholesky | solution.py:58
  427.4 10.6 %custom-call.11 = f32[1,128,128]{1,2,0:T(8,128)S(1)} custom-call(f32[1,128,128]{2,1,0:T(8,128)} %fusion.27), custom_call_target="InvertDiagBlocksLowerTriangular" | custom-call | tf_op jit(solution)/shard_map/jit(_solve_triangular)/triangular_solve | solution.py:59
  442.9 10.7 %psum.46 = f32[128]{0:T(128)S(1)} all-reduce(f32[128]{0:T(128)} %fusion.14), channel_id=1, replica_groups=mesh['parts'=2,'tm'=4,'factor'=4] {'tm'}, use_global_device_ids=true, to_apply=%region_6.9 | all-reduce | flops 128 | bytes 1024 | tf_op jit(solution)/shard_map/psum | solution.py:57
  456.9 8.7 %psum.47 = f32[128]{0:T(128)S(1)} all-reduce(f32[128]{0:T(128)S(1)} %fusion.13), channel_id=1, replica_groups=mesh['parts'=2,'tm'=4,'factor'=4] {'tm'}, use_global_device_ids=true, to_apply=%region_7.11 | all-reduce | flops 128 | bytes 1024 | tf_op jit(solution)/shard_map/psum | solution.py:57
  475.3 3.9 collective-permute-start.2
  480.9 75.3 %all-gather.5.cloned.1.call-done = f32[12288,128]{0,1:T(8,128)} async-done(((f32[3072,128]{0,1:T(8,128)}), f32[12288,128]{0,1:T(8,128)}) %all-gather.5.cloned.1.call-update) | async-done | bytes 6291472 | tf_op jit(solution)/shard_map/all_gather | solution.py:63
  556.2 8.3 %reshape.110 = f32[24,4,128,128]{2,1,0,3:T(4,128)} reshape(f32[12288,128]{0,1:T(8,128)} %all-gather.5.cloned.1.call-done) | data formatting | bytes 12582912 | tf_op jit(solution)/shard_map/reshape | solution.py:64
  564.5 5.6 constant_dynamic-slice_fusion
  573.8 37.3 %bitcast_subtract_fusion = f32[3072,24,1,128]{3,0,1,2:T(8,128)} fusion(f32[3072,24,1,128]{3,0,1,2:T(8,128)} %bitcast_subtract_fusion.1, f32[24,1,128,128]{3,2,0,1:T(8,128)S(1)} %copy.19, f32[128,3072]{1,0:T(8,128)S(1)} %copy-done.2), kind=kOutput, calls=%fused_computation | convolution fusion | flops 14504951808 | bytes 78643200 | tf_op jit(solution)/shard_map/rk,tck->rtc/dot_general | solution.py:68
  611.1 43.3 %copy.21 = f32[3072,24,1,128]{3,2,1,0:T(1,128)} copy(f32[3072,24,1,128]{3,0,1,2:T(8,128)} %bitcast_subtract_fusion) | data formatting | bytes 75497472
  (81 shorter events, 39.6 us)
Async XLA Ops:
  7.2 459.6 %copy-start = (f32[1,256,256]{2,1,0:T(8,128)S(1)}, f32[1,256,256]{2,1,0:T(8,128)}, u32[]{:S(2)}) copy-start(f32[1,256,256]{2,1,0:T(8,128)} %param.18) | copy-start | bytes 786436
  7.2 81.4 %all-reduce.5.cloned.1.call-start = ((), (), s32[]{:S(2)}) async-start(), calls=%async_computation | async-start | bytes 3145728 | tf_op jit(solution)/shard_map/psum | solution.py:13
  42.9 83.9 %all-reduce.7.cloned.1.call-start = ((), (), s32[]{:S(2)}) async-start(), calls=%async_computation.1 | async-start | bytes 131072 | tf_op jit(solution)/shard_map/psum | solution.py:57
  88.6 62.9 %copy-start.4 = (f32[3072,128]{1,0:T(8,128)S(1)}, f32[3072,128]{1,0:T(8,128)}, u32[]{:S(2)}) copy-start(f32[3072,128]{1,0:T(8,128)} %all-reduce.5.cloned.1.call-done) | copy-start | bytes 4718596
  92.6 176.8 %all-gather.3.cloned.1.call-start = ((), (), s32[]{:S(2)}) async-start(), calls=%async_computation.2 | async-start | bytes 7864320 | tf_op jit(solution)/shard_map/all_gather | solution.py:63
  154.1 218.1 %all-reduce.9.cloned.1.call-start = ((), (), s32[]{:S(2)}) async-start(), calls=%async_computation.3 | async-start | bytes 3145728 | tf_op jit(solution)/shard_map/psum | solution.py:13
  283.2 3.9 copy-start.3
  331.0 79.4 %all-reduce.11.cloned.1.call-start = ((), (), s32[]{:S(2)}) async-start(), calls=%async_computation.4 | async-start | bytes 131072 | tf_op jit(solution)/shard_map/psum | solution.py:57
  331.1 45.4 %copy-start.6 = (s32[3072]{0:T(1024)}, s32[3072]{0:T(1024)S(1)}, u32[]{:S(2)}) copy-start(s32[3072]{0:T(1024)S(1)} %fusion.36) | copy-start | bytes 36868
  372.2 65.8 %copy-start.5 = (f32[3072,128]{1,0:T(8,128)S(1)}, f32[3072,128]{1,0:T(8,128)}, u32[]{:S(2)}) copy-start(f32[3072,128]{1,0:T(8,128)} %all-reduce.9.cloned.1.call-done) | copy-start | bytes 4718596
  376.2 180.0 %all-gather.5.cloned.1.call-start = ((), (), s32[]{:S(2)}) async-start(), calls=%async_computation.5 | async-start | bytes 7864320 | tf_op jit(solution)/shard_map/all_gather | solution.py:63
  440.7 25.0 %copy-start.9 = (f32[1,256]{1,0:T(1,128)S(1)}, f32[1,256]{1,0:T(1,128)}, u32[]{:S(2)}) copy-start(f32[1,256]{1,0:T(1,128)} %param.15) | copy-start | bytes 3076
  440.7 30.9 %copy-start.2 = (f32[128,3072]{1,0:T(8,128)S(1)}, f32[128,3072]{1,0:T(8,128)}, u32[]{:S(2)}) copy-start(f32[128,3072]{1,0:T(8,128)} %convolution_select_fusion) | copy-start | bytes 4718596
  454.7 18.5 %copy-start.7 = (f32[1,2,256]{2,1,0:T(2,128)S(1)}, f32[1,2,256]{2,1,0:T(2,128)}, u32[]{:S(2)}) copy-start(f32[1,2,256]{2,1,0:T(2,128)} %param.20) | copy-start | bytes 6148
  454.7 18.6 %copy-start.8 = (f32[1,2,256]{2,1,0:T(2,128)S(1)}, f32[1,2,256]{2,1,0:T(2,128)}, u32[]{:S(2)}) copy-start(f32[1,2,256]{2,1,0:T(2,128)} %param.19) | copy-start | bytes 6148
  467.3 5.9 collective-permute-start.1
  468.6 4.7 collective-permute-start
  474.0 5.2 collective-permute-start.3
  475.3 4.5 collective-permute-start.2
  611.1 43.3 %copy-start.1 = (f32[1,256,256]{2,1,0:T(8,128)S(1)}, f32[1,256,256]{2,1,0:T(8,128)}, u32[]{:S(2)}) copy-start(f32[1,256,256]{2,1,0:T(8,128)} %param.18) | copy-start | bytes 786436
Sparse Core Ops, SparseCore 0:
  43.0 45.5 all-reduce.4
  92.7 34.0 all-reduce.6
  154.3 115.0 all-gather.2
  331.1 41.0 all-reduce.8
  376.4 34.0 all-reduce.10
  440.8 115.3 all-gather.4
where the time goes:
time: 671 us; the launch traced here: 662 us
  waiting for transfers between devices  345 us (51%)
  local copies, waits for them, and re-layouts  114 us (17%)
  matrix products  101 us (15%)
  other arithmetic  57.2 us (9%)
  blocking collectives  19.4 us (3%)
  between operations  14.7 us (2%)
  starting transfers between devices  10.4 us (2%)
    all_gather x2, waiting for transfers between devices, shards(): all_factor = lax.all_gather(factor_rows, 'tm', axis=0, tiled=True)  190 us
    psum x2, waiting for transfers between devices, spread(): return lax.psum(jnp.where(mine, array, jnp.zeros_like(array)), axis)  86.8 us
    dot_general x2, matrix products, shards(): jnp.einsum('rk,tck->rtc', factor_rows, my_tiles, precision=lax.Precision....  78.5 us
    unnamed x22, local copies, waits for them, and re-layouts  76.3 us
    psum x2, waiting for transfers between devices, shards(): diag_block, rhs_segment = lax.psum((block_part, rhs_part), 'tm')  68.1 us
    another operation x6, other arithmetic, shards(): lower_block = jnp.linalg.cholesky(diag_block)  25.6 us
    another operation x4, other arithmetic, shards(): jax.scipy.linalg.solve_triangular(lower_block, panel_cols.T, lower=True)  22.4 us
    psum x2, blocking collectives, shards(): diag_block, rhs_segment = lax.psum((block_part, rhs_part), 'tm')  19.4 us
  transfers between devices with their start and end apart: 10, of which 7 were waited for; matrix products, arithmetic and copies ran while one was open for 2% of the time, Pallas kernels for 0%

commit v1 on v0

--- a/solution.py
+++ b/solution.py
@@ -60,7 +60,27 @@
         factor_rows = jnp.where(
             (global_rows < panel_first)[:, None], jnp.zeros_like(factor_rows), factor_rows
         )
-        all_factor = lax.all_gather(factor_rows, "tm", axis=0, tiled=True)
+        out_arr = lax.axis_size("tm")
+        frame_out = lax.axis_index("tm")
+        met_up, known, aux = (out_arr, frame_out, factor_rows.shape[0])
+        queue = tuple(
+            (dev_j * met_up if t == 0 else dev_j for t, dev_j in enumerate(factor_rows.shape))
+        )
+        back = jnp.zeros(queue, factor_rows.dtype)
+        all_factor = lax.dynamic_update_slice_in_dim(back, factor_rows, known * aux, axis=0)
+        mixed_arr = opened = factor_rows
+        for u in range(1, met_up // 2 + 1):
+            piece_next = tuple(((t, (t + 1) % met_up) for t in range(met_up)))
+            mixed_arr = lax.ppermute(mixed_arr, axis_name="tm", perm=piece_next)
+            all_factor = lax.dynamic_update_slice_in_dim(
+                all_factor, mixed_arr, (known - u) % met_up * aux, axis=0
+            )
+            if 2 * u < met_up:
+                now = tuple(((t, (t - 1) % met_up) for t in range(met_up)))
+                opened = lax.ppermute(opened, axis_name="tm", perm=now)
+                all_factor = lax.dynamic_update_slice_in_dim(
+                    all_factor, opened, (known + u) % met_up * aux, axis=0
+                )
         grouped = all_factor.reshape(tiles_here, factors, width, width)
         my_tiles = lax.dynamic_index_in_dim(grouped, factor_here, 1, keepdims=False)
         link_step = jax.scipy.linalg.solve_triangular(lower_block, rhs_segment, lower=True)

time: 671 us -> 625 us (0.931)
  the two profiles are of different devices: /device:TPU:0 before, /device:TPU:16 now
where the time goes in v1:
time: 625 us; the launch traced here: 616 us
  waiting for transfers between devices  308 us (49%)
  local copies, waits for them, and re-layouts  108 us (17%)
  matrix products  102 us (16%)
  other arithmetic  53.6 us (9%)
  blocking collectives  17.4 us (3%)
  between operations  14.3 us (2%)
  starting transfers between devices  13.7 us (2%)
    ppermute x4, waiting for transfers between devices, shards(): mixed_arr = lax.ppermute(mixed_arr, axis_name='tm', perm=piece_next)  122 us
    dot_general x2, matrix products, shards(): jnp.einsum('rk,tck->rtc', factor_rows, my_tiles, precision=lax.Precision....  84.6 us
    unnamed x28, local copies, waits for them, and re-layouts  78.9 us
    psum x2, waiting for transfers between devices, spread(): return lax.psum(jnp.where(mine, array, jnp.zeros_like(array)), axis)  76.1 us
    psum x2, waiting for transfers between devices, shards(): diag_block, rhs_segment = lax.psum((block_part, rhs_part), 'tm')  58.1 us
    ppermute x2, waiting for transfers between devices, with_halo(): lax.ppermute(tail, axis, [(i, (i + 1) % count) for i in range(ends)])  51.6 us
    another operation x6, other arithmetic, shards(): lower_block = jnp.linalg.cholesky(diag_block)  24.8 us
    another operation x4, other arithmetic, shards(): jax.scipy.linalg.solve_triangular(lower_block, panel_cols.T, lower=True)  20.9 us
  transfers between devices with their start and end apart: 14, of which 9 were waited for; matrix products, arithmetic and copies ran while one was open for 4% of the time, Pallas kernels for 0%

profile of v1, /device:TPU:16, one launch (start us, length us, event | category | flops | bytes accessed | tf_op | source)
XLA Modules:
  0.0 616.0 jit_solution(1532008256796375847)
XLA Ops:
  7.2 32.9 %copy.28 = f32[3072,24,1,128]{3,0,1,2:T(8,128)} copy(f32[3072,24,1,128]{3,2,1,0:T(1,128)} %param.13) | data formatting | bytes 75497472 | tf_op args[0]
  42.9 44.0 %all-reduce.5.cloned.1.call-done = f32[3072,128]{1,0:T(8,128)} async-done(((f32[3072,128]{1,0:T(8,128)}), f32[3072,128]{1,0:T(8,128)}) %all-reduce.5.cloned.1.call-update) | async-done | bytes 1572880 | tf_op jit(solution)/shard_map/psum | solution.py:13
  86.9 4.0 fusion.10
  91.0 33.9 %all-reduce.7.cloned.1.call-done = f32[128,128]{0,1:T(8,128)} async-done(((f32[128,128]{0,1:T(8,128)}), f32[128,128]{0,1:T(8,128)}) %all-reduce.7.cloned.1.call-update) | async-done | bytes 65552 | tf_op jit(solution)/shard_map/psum | solution.py:57
  126.7 11.7 %cholesky.44 = f32[128,128]{1,0:T(8,128)S(1)} custom-call(f32[128,128]{1,0:T(8,128)S(1)} %fusion.37), custom_call_target="Cholesky" | custom-call | tf_op jit(solution)/shard_map/jit(cholesky)/cholesky | solution.py:58
  139.7 9.8 %custom-call.10 = f32[1,128,128]{1,2,0:T(8,128)S(1)} custom-call(f32[1,128,128]{2,1,0:T(8,128)S(1)} %fusion.28), custom_call_target="InvertDiagBlocksLowerTriangular" | custom-call | tf_op jit(solution)/shard_map/jit(_solve_triangular)/triangular_solve | solution.py:59
  153.6 65.3 %collective-permute-done = f32[3072,128]{0,1:T(8,128)} collective-permute-done((f32[3072,128]{0,1:T(8,128)S(1)}, f32[3072,128]{0,1:T(8,128)}, u32[]{:S(2)}, u32[]{:S(2)}) %collective-permute-start) | collective-permute-done | bytes 1572896 | tf_op jit(solution)/shard_map/ppermute | solution.py:74
  219.3 2.9 broadcast.115.clone
  225.3 3.0 copy.25
  231.6 21.3 %collective-permute-done.2 = f32[3072,128]{0,1:T(8,128)} collective-permute-done((f32[3072,128]{0,1:T(8,128)}, f32[3072,128]{0,1:T(8,128)}, u32[]{:S(2)}, u32[]{:S(2)}) %collective-permute-start.2) | collective-permute-done | bytes 1572896 | tf_op jit(solution)/shard_map/ppermute | solution.py:74
  256.0 46.5 %bitcast_subtract_fusion.1 = f32[3072,24,1,128]{3,0,1,2:T(8,128)} fusion(f32[128,3072]{1,0:T(8,128)S(1)} %convolution_select_fusion.1, f32[24,4,128,128]{3,2,1,0:T(8,128)} %bitcast.7, s32[]{:T(128)S(6)} %select_n.90, f32[3072,24,1,128]{3,2,1,0:T(1,128)} %param.13), kind=kOutput, calls=%fused_computation.1 | convolution fusion | flops 14504951808 | bytes 78643200 | tf_op jit(solution)/shard_map/rk,tck->rtc/dot_general | solution.py:88
  306.7 8.5 %psum.46 = f32[128]{0:T(128)S(1)} all-reduce(f32[128]{0:T(128)S(1)} %fusion.16), channel_id=1, replica_groups=mesh['parts'=2,'tm'=4,'factor'=4] {'tm'}, use_global_device_ids=true, to_apply=%region_6.9 | all-reduce | flops 128 | bytes 1024 | tf_op jit(solution)/shard_map/psum | solution.py:57
  316.3 32.1 %all-reduce.9.cloned.1.call-done = f32[3072,128]{1,0:T(8,128)} async-done(((f32[3072,128]{1,0:T(8,128)}), f32[3072,128]{1,0:T(8,128)}) %all-reduce.9.cloned.1.call-update) | async-done | bytes 1572880 | tf_op jit(solution)/shard_map/psum | solution.py:13
  348.4 4.0 fusion.11
  353.2 8.9 %psum.47 = f32[128]{0:T(128)S(1)} all-reduce(f32[128]{0:T(128)S(1)} %fusion.15), channel_id=1, replica_groups=mesh['parts'=2,'tm'=4,'factor'=4] {'tm'}, use_global_device_ids=true, to_apply=%region_7.11 | all-reduce | flops 128 | bytes 1024 | tf_op jit(solution)/shard_map/psum | solution.py:57
  362.1 24.2 %all-reduce.11.cloned.1.call-done = f32[128,128]{0,1:T(8,128)} async-done(((f32[128,128]{0,1:T(8,128)}), f32[128,128]{0,1:T(8,128)}) %all-reduce.11.cloned.1.call-update) | async-done | bytes 65552 | tf_op jit(solution)/shard_map/psum | solution.py:57
  388.1 11.7 %cholesky.55 = f32[128,128]{1,0:T(8,128)S(1)} custom-call(f32[128,128]{1,0:T(8,128)S(1)} %fusion.33), custom_call_target="Cholesky" | custom-call | tf_op jit(solution)/shard_map/jit(cholesky)/cholesky | solution.py:58
  401.2 9.8 %custom-call.11 = f32[1,128,128]{1,2,0:T(8,128)S(1)} custom-call(f32[1,128,128]{2,1,0:T(8,128)S(1)} %fusion.29), custom_call_target="InvertDiagBlocksLowerTriangular" | custom-call | tf_op jit(solution)/shard_map/jit(_solve_triangular)/triangular_solve | solution.py:59
  423.5 21.3 %collective-permute-done.6 = f32[1,4]{1,0:T(1,128)S(1)} collective-permute-done((f32[1,4]{1,0:T(1,128)S(1)}, f32[1,4]{1,0:T(1,128)S(1)}, u32[]{:S(2)}, u32[]{:S(2)}) %collective-permute-start.6) | collective-permute-done | bytes 48 | tf_op jit(solution)/shard_map/ppermute | solution.py:24
  445.3 35.2 %collective-permute-done.3 = f32[3072,128]{0,1:T(8,128)} collective-permute-done((f32[3072,128]{0,1:T(8,128)S(1)}, f32[3072,128]{0,1:T(8,128)}, u32[]{:S(2)}, u32[]{:S(2)}) %collective-permute-start.3) | collective-permute-done | bytes 1572896 | tf_op jit(solution)/shard_map/ppermute | solution.py:74
  485.1 30.2 %collective-permute-done.8 = f32[1,4]{1,0:T(1,128)S(1)} collective-permute-done((f32[1,4]{1,0:T(1,128)S(1)}, f32[1,4]{1,0:T(1,128)S(1)}, u32[]{:S(2)}, u32[]{:S(2)}) %collective-permute-start.8) | collective-permute-done | bytes 48 | tf_op jit(solution)/shard_map/ppermute | solution.py:24
  518.4 3.0 copy.33
  527.8 38.1 %bitcast_subtract_fusion = f32[3072,24,1,128]{3,0,1,2:T(8,128)} fusion(f32[3072,24,1,128]{3,0,1,2:T(8,128)} %bitcast_subtract_fusion.1, f32[128,3072]{1,0:T(8,128)S(1)} %convolution_select_fusion, f32[24,4,128,128]{3,2,1,0:T(8,128)} %bitcast.150, s32[]{:T(128)S(6)} %select_n.90), kind=kOutput, calls=%fused_computation | convolution fusion | flops 14504951808 | bytes 78643200 | tf_op jit(solution)/shard_map/rk,tck->rtc/dot_general | solution.py:88
  566.0 43.3 %copy.36 = f32[3072,24,1,128]{3,2,1,0:T(1,128)} copy(f32[3072,24,1,128]{3,0,1,2:T(8,128)} %bitcast_subtract_fusion) | data formatting | bytes 75497472
  (105 shorter events, 55.9 us)
Async XLA Ops:
  7.2 406.5 %copy-start = (f32[1,256,256]{2,1,0:T(8,128)S(1)}, f32[1,256,256]{2,1,0:T(8,128)}, u32[]{:S(2)}) copy-start(f32[1,256,256]{2,1,0:T(8,128)} %param.18) | copy-start | bytes 786436
  7.2 79.7 %all-reduce.5.cloned.1.call-start = ((), (), s32[]{:S(2)}) async-start(), calls=%async_computation | async-start | bytes 3145728 | tf_op jit(solution)/shard_map/psum | solution.py:13
  42.9 82.0 %all-reduce.7.cloned.1.call-start = ((), (), s32[]{:S(2)}) async-start(), calls=%async_computation.1 | async-start | bytes 131072 | tf_op jit(solution)/shard_map/psum | solution.py:57
  86.9 62.6 %copy-start.4 = (f32[3072,128]{1,0:T(8,128)S(1)}, f32[3072,128]{1,0:T(8,128)}, u32[]{:S(2)}) copy-start(f32[3072,128]{1,0:T(8,128)} %all-reduce.5.cloned.1.call-done) | copy-start | bytes 4718596
  91.0 257.4 %all-reduce.9.cloned.1.call-start = ((), (), s32[]{:S(2)}) async-start(), calls=%async_computation.2 | async-start | bytes 3145728 | tf_op jit(solution)/shard_map/psum | solution.py:13
  151.1 67.8 %collective-permute-start = (f32[3072,128]{0,1:T(8,128)S(1)}, f32[3072,128]{0,1:T(8,128)}, u32[]{:S(2)}, u32[]{:S(2)}) collective-permute-start(f32[3072,128]{0,1:T(8,128)S(1)} %bitcast.144), channel_id=1, source_target_pairs={{0,4},{4,8},{8,12},{12,0},{1,5},{5,9},{9,13},{13,1},{2,6},{6,10},{... | collective-permute-start | bytes 4718600 | tf_op jit(solution)/shard_map/ppermute | solution.py:74
  151.7 73.7 %collective-permute-start.1 = (f32[3072,128]{0,1:T(8,128)S(1)}, f32[3072,128]{0,1:T(8,128)}, u32[]{:S(2)}, u32[]{:S(2)}) collective-permute-start(f32[3072,128]{0,1:T(8,128)S(1)} %bitcast.145), channel_id=1, source_target_pairs={{0,12},{4,0},{8,4},{12,8},{1,13},{5,1},{9,5},{13,9},{2,14},{6,2},{... | collective-permute-start | bytes 4718600 | tf_op jit(solution)/shard_map/ppermute | solution.py:80
  218.9 34.0 %collective-permute-start.2 = (f32[3072,128]{0,1:T(8,128)}, f32[3072,128]{0,1:T(8,128)}, u32[]{:S(2)}, u32[]{:S(2)}) collective-permute-start(f32[3072,128]{0,1:T(8,128)} %collective-permute-done), channel_id=1, source_target_pairs={{0,4},{4,8},{8,12},{12,0},{1,5},{5,9},{9,13},{13,1},{2,6},{6,10},{... | collective-permute-start | bytes 4718600 | tf_op jit(solution)/shard_map/ppermute | solution.py:74
  228.4 2.0 copy-start.6
  305.2 81.2 %all-reduce.11.cloned.1.call-start = ((), (), s32[]{:S(2)}) async-start(), calls=%async_computation.3 | async-start | bytes 131072 | tf_op jit(solution)/shard_map/psum | solution.py:57
  348.4 62.8 %copy-start.3 = (f32[3072,128]{1,0:T(8,128)S(1)}, f32[3072,128]{1,0:T(8,128)}, u32[]{:S(2)}) copy-start(f32[3072,128]{1,0:T(8,128)} %all-reduce.9.cloned.1.call-done) | copy-start | bytes 4718596
  411.2 2.2 copy-start.10
  411.2 2.2 copy-start.11
  411.2 2.2 copy-start.12
  412.7 67.8 %collective-permute-start.3 = (f32[3072,128]{0,1:T(8,128)S(1)}, f32[3072,128]{0,1:T(8,128)}, u32[]{:S(2)}, u32[]{:S(2)}) collective-permute-start(f32[3072,128]{0,1:T(8,128)S(1)} %bitcast.147), channel_id=1, source_target_pairs={{0,4},{4,8},{8,12},{12,0},{1,5},{5,9},{9,13},{13,1},{2,6},{6,10},{... | collective-permute-start | bytes 4718600 | tf_op jit(solution)/shard_map/ppermute | solution.py:74
  414.2 8.7 %collective-permute-start.7 = (f32[1,4]{1,0:T(1,128)S(1)}, f32[1,4]{1,0:T(1,128)S(1)}, u32[]{:S(2)}, u32[]{:S(2)}) collective-permute-start(f32[1,4]{1,0:T(1,128)S(1)} %pad_maximum_fusion.1), channel_id=1, source_target_pairs={{1,0},{2,1},{3,2},{4,3},{5,4},{6,5},{7,6},{8,7},{9,8},{10,9},{11,1... | collective-permute-start | bytes 56 | tf_op jit(solution)/shard_map/ppermute | solution.py:26
  416.1 28.7 %collective-permute-start.6 = (f32[1,4]{1,0:T(1,128)S(1)}, f32[1,4]{1,0:T(1,128)S(1)}, u32[]{:S(2)}, u32[]{:S(2)}) collective-permute-start(f32[1,4]{1,0:T(1,128)S(1)} %pad_maximum_fusion.1), channel_id=1, source_target_pairs={{0,1},{1,2},{2,3},{3,4},{4,5},{5,6},{6,7},{7,8},{8,9},{9,10},{10,1... | collective-permute-start | bytes 56 | tf_op jit(solution)/shard_map/ppermute | solution.py:24
  419.0 99.4 %collective-permute-start.4 = (f32[3072,128]{0,1:T(8,128)S(1)}, f32[3072,128]{0,1:T(8,128)}, u32[]{:S(2)}, u32[]{:S(2)}) collective-permute-start(f32[3072,128]{0,1:T(8,128)S(1)} %bitcast.149), channel_id=1, source_target_pairs={{0,12},{4,0},{8,4},{12,8},{1,13},{5,1},{9,5},{13,9},{2,14},{6,2},{... | collective-permute-start | bytes 4718600 | tf_op jit(solution)/shard_map/ppermute | solution.py:80
  422.7 22.1 %copy-start.9 = (f32[1,2,256]{2,1,0:T(2,128)S(1)}, f32[1,2,256]{2,1,0:T(2,128)}, u32[]{:S(2)}) copy-start(f32[1,2,256]{2,1,0:T(2,128)} %param.19) | copy-start | bytes 6148
  422.8 57.7 %copy-start.2 = (f32[12288,128]{1,0:T(8,128)}, f32[12288,128]{1,0:T(8,128)S(1)}, u32[]{:S(2)}) copy-start(f32[12288,128]{1,0:T(8,128)S(1)} %constant_dynamic-update-slice_fusion.3) | copy-start | bytes 18874372
  480.5 44.2 %collective-permute-start.5 = (f32[3072,128]{0,1:T(8,128)}, f32[3072,128]{0,1:T(8,128)}, u32[]{:S(2)}, u32[]{:S(2)}) collective-permute-start(f32[3072,128]{0,1:T(8,128)} %collective-permute-done.3), channel_id=1, source_target_pairs={{0,4},{4,8},{8,12},{12,0},{1,5},{5,9},{9,13},{13,1},{2,6},{6,10},{... | collective-permute-start | bytes 4718600 | tf_op jit(solution)/shard_map/ppermute | solution.py:74
  480.7 4.3 collective-permute-start.9
  482.6 32.8 %collective-permute-start.8 = (f32[1,4]{1,0:T(1,128)S(1)}, f32[1,4]{1,0:T(1,128)S(1)}, u32[]{:S(2)}, u32[]{:S(2)}) collective-permute-start(f32[1,4]{1,0:T(1,128)S(1)} %pad_maximum_fusion.2), channel_id=1, source_target_pairs={{0,1},{1,2},{2,3},{3,4},{4,5},{5,6},{6,7},{7,8},{8,9},{9,10},{10,1... | collective-permute-start | bytes 56 | tf_op jit(solution)/shard_map/ppermute | solution.py:24
  566.0 43.3 %copy-start.1 = (f32[1,256,256]{2,1,0:T(8,128)S(1)}, f32[1,256,256]{2,1,0:T(8,128)}, u32[]{:S(2)}) copy-start(f32[1,256,256]{2,1,0:T(8,128)} %param.18) | copy-start | bytes 786436
  (3 other events, 3.4 us)
Sparse Core Ops, SparseCore 0:
  43.0 43.9 all-reduce.4
  91.1 33.7 all-reduce.6
  305.3 43.0 all-reduce.8
  352.5 33.7 all-reduce.10
